TPU v7x, 32 devices: a whole 2x2x4 slice. The times are simulated.
32 devices in a mesh: row: 8 (over z, x), col: 4 (over y, core).
Axes of the slice: x: 2, y: 2, z: 4, core: 2. Of those that a mesh axis runs over, the one named last changes fastest.
Arguments:
- vectors: float32 [64, 4096], P(None, ('row', 'col')), may hold values from -6 to 6
- blocks: bfloat16 [8, 4, 152, 128, 128], P('row', 'col'), may hold values from -0.0390625 to 0.0390625
- slot_block_rows: int32 [8, 4, 152], P('row', 'col'), may hold values from 0 to 3
- slot_block_columns: int32 [8, 4, 152], P('row', 'col'), may hold values from 0 to 7
- counts: int32 [8, 4], P('row', 'col'), may hold values from 38 to 152, as said below
Outputs:
- filtered: float32 [64, 4096], P(None, ('row', 'col'))
Inputs may be any that keep to these rules, and one draw needn't show every extreme that they name: `counts`: slots at or after a device's count carry no block.
All inputs are finite; a program needn't handle non-finite values.
Results may differ from a plain program's by a relative error of at most 0.023.
Values may be sent and summed in bfloat16 or wider, within the bound.
A program may use at most 64 MiB of HBM per device.

v0:
```python
import jax
import jax.numpy as jnp
from jax import lax
from jax.sharding import PartitionSpec as P

DEGREE = 3


CENTER = 0.25
HALF_WIDTH = 2.0


def local(vectors, blocks, slot_block_rows, slot_block_columns, counts):
    width, piece_rows = vectors.shape
    block_entries = blocks[0, 0]
    rows_here = slot_block_rows[0, 0]
    cols_here = slot_block_columns[0, 0]
    live_count = counts[0, 0]
    slot_total = block_entries.shape[0]
    block_size = block_entries.shape[1]
    row_count = lax.axis_size("row")
    col_count = lax.axis_size("col")
    slab_groups = row_count // col_count
    row_index = lax.axis_index("row")
    col_index = lax.axis_index("col")
    slab_blocks = col_count * piece_rows // block_size
    col_blocks = slab_groups * slab_blocks
    slot_numbers = jnp.arange(slot_total, dtype=jnp.int32)
    global_rows = row_index * slab_blocks + rows_here
    global_cols = (
        col_index + col_count * (cols_here // slab_blocks)
    ) * slab_blocks + cols_here % slab_blocks
    live = (slot_numbers < live_count) & (global_rows <= global_cols)
    values_live = jnp.where(live[:, None, None], block_entries, jnp.zeros_like(block_entries))
    onehot_rows = (rows_here[:, None] == jnp.arange(slab_blocks, dtype=jnp.int32)[None, :]).astype(
        jnp.float32
    )
    onehot_cols = (cols_here[:, None] == jnp.arange(col_blocks, dtype=jnp.int32)[None, :]).astype(
        jnp.float32
    )

    def hamiltonian(current):
        wire = current.astype(jnp.bfloat16)
        row_slab = lax.all_gather(wire, "col", axis=1, tiled=True)
        stacked = lax.all_gather(wire, "row", axis=1, tiled=True)
        col_slab = lax.all_to_all(
            stacked.reshape(width, slab_groups, col_count, piece_rows),
            "col",
            split_axis=2,
            concat_axis=2,
            tiled=True,
        )
        col_slab = col_slab.reshape(width, col_blocks * block_size)
        inputs_col = col_slab.reshape(width, col_blocks, block_size)[:, cols_here, :]
        products = jnp.einsum(
            "sab,ksb->ksa", values_live, inputs_col, preferred_element_type=jnp.float32
        )
        row_part = jnp.einsum("sr,ksa->kra", onehot_rows, products)
        inputs_row = row_slab.reshape(width, slab_blocks, block_size)[:, rows_here, :]
        products_t = jnp.einsum(
            "sba,ksb->ksa", values_live, inputs_row, preferred_element_type=jnp.float32
        )
        col_part = jnp.einsum("sc,ksa->kca", onehot_cols, products_t)
        col_wire = col_part.astype(jnp.bfloat16).reshape(width, slab_groups, col_count, piece_rows)
        row_bf = row_part.astype(jnp.bfloat16)
        row_wire = row_bf.reshape(width, 1, col_count, piece_rows)
        row_received, received = (
            lax.all_to_all(row_wire, "col", split_axis=2, concat_axis=2, tiled=True),
            lax.all_to_all(col_wire, "col", split_axis=2, concat_axis=2, tiled=True),
        )
        row_total = jnp.sum(row_received.astype(jnp.float32), axis=(1, 2))
        flat_terms = received.reshape(width, row_count * piece_rows)
        col_total = lax.psum_scatter(flat_terms, "row", scatter_dimension=1, tiled=True).astype(
            jnp.float32
        )
        return row_total + col_total

    previous = vectors
    current = (hamiltonian(vectors) - CENTER * vectors) / HALF_WIDTH
    for degree_step in range(DEGREE - 1):
        image = hamiltonian(current)
        following = 2.0 * (image - CENTER * current) / HALF_WIDTH - previous
        previous, current = (current, following)
    return current


def solution(mesh):
    in_specs = (
        P(None, ("row", "col")),
        P("row", "col", None, None, None),
        P("row", "col", None),
        P("row", "col", None),
        P("row", "col"),
    )
    out_specs = P(None, ("row", "col"))
    return jax.shard_map(local, mesh=mesh, in_specs=in_specs, out_specs=out_specs, check_vma=False)
```

profile of v0, /device:TPU:0, one launch (start us, length us, event | category | flops | bytes accessed | tf_op | source)
XLA Modules:
  0.0 367.6 jit_solution(17402253800268710777)
XLA Ops:
  6.5 0.8 convert_element_type.65
  7.3 27.9 %all_gather.18 = bf16[64,1024]{1,0:T(8,128)(2,1)S(1)} all-gather(bf16[64,128]{1,0:T(8,128)(2,1)S(1)} %convert_element_type.65), channel_id=1, replica_groups=mesh['row'=8,'col'=4] {'row'}, dimensions={1}, use_global_device_ids=true | all-gather | bytes 147456 | tf_op jit(solution)/shard_map/all_gather | solution.py:45
  35.2 0.1 reshape.166
  35.3 0.7 copy.41
  35.9 3.3 all-to-all-start
  39.3 5.8 %all_gather.19 = bf16[64,512]{1,0:T(8,128)(2,1)S(1)} all-gather(bf16[64,128]{1,0:T(8,128)(2,1)S(1)} %convert_element_type.65), channel_id=1, replica_groups=mesh['row'=8,'col'=4] {'col'}, dimensions={1}, use_global_device_ids=true | all-gather | bytes 81920 | tf_op jit(solution)/shard_map/all_gather | solution.py:44
  45.7 0.7 compare_select_fusion.1
  46.4 0.7 compare_select_fusion
  47.1 0.0 copy-start.1
  47.1 0.0 copy-start.2
  47.1 1.0 gather_fusion.1
  48.2 3.9 %fusion.27 = bf16[64,152,128]{2,0,1:T(8,128)(2,1)S(1)} fusion(bf16[152,64,128]{2,1,0:T(8,128)(2,1)S(1)} %gather_fusion.1, bf16[1,1,152,128,128]{4,3,2,1,0:T(8,128)(2,1)} %param.6, pred[152]{0:T(512)(128)(4,1)S(1)} %compare_and_fusion), kind=kOutput, calls=%fused_computation.32 | convolution fusion | flops 321257472 | bytes 9961624 | tf_op jit(solution)/shard_map/sba,ksb->ksa/dot_general | solution.py:60
  52.2 1.4 fusion.42
  53.6 0.7 copy.47
  54.3 0.0 all-to-all-done
  54.3 3.3 all-to-all-start.2
  57.7 0.0 reduce-scatter.10.cloned.1.call-start
  57.7 1.0 gather_fusion
  58.8 7.4 %fusion.24 = bf16[64,152,128]{2,0,1:T(8,128)(2,1)} fusion(bf16[152,64,128]{2,1,0:T(8,128)(2,1)S(1)} %gather_fusion, bf16[1,1,152,128,128]{4,3,2,1,0:T(8,128)(2,1)} %param.6, pred[152]{0:T(512)(128)(4,1)S(1)} %compare_and_fusion), kind=kOutput, calls=%fused_computation.31 | convolution fusion | flops 321257472 | bytes 9961624 | tf_op jit(solution)/shard_map/sab,ksb->ksa/dot_general | solution.py:55
  66.2 0.9 copy.71
  67.0 0.0 reduce-scatter.10.cloned.1.call-update
  67.1 3.1 fusion.66
  70.2 7.1 %all_to_all.45 = bf16[64,1,4,128]{3,0,1,2:T(8,128)(2,1)S(1)} all-to-all(bf16[64,1,4,128]{3,0,1,2:T(8,128)(2,1)S(1)} %copy.44), channel_id=1, replica_groups=mesh['row'=8,'col'=4] {'col'}, dimensions={2} | all-to-all | bytes 131072 | tf_op jit(solution)/shard_map/all_to_all | solution.py:68
  77.3 50.8 %reduce-scatter.10.cloned.1.call-done = bf16[128,64]{1,0:T(8,128)(2,1)} async-done(((bf16[1024,64]{1,0:T(8,128)(2,1)}), bf16[128,64]{1,0:T(8,128)(2,1)}) %reduce-scatter.10.cloned.1.call-update) | async-done | bytes 16400
  128.2 0.8 copy.66
  129.1 26.2 %all_gather.20 = bf16[64,1024]{1,0:T(8,128)(2,1)S(1)} all-gather(bf16[64,128]{1,0:T(8,128)(2,1)S(1)} %multiply_convert_fusion), channel_id=1, replica_groups=mesh['row'=8,'col'=4] {'row'}, dimensions={1}, use_global_device_ids=true | all-gather | bytes 147456 | tf_op jit(solution)/shard_map/all_gather | solution.py:45
  155.2 5.3 %all_gather.21 = bf16[64,512]{1,0:T(8,128)(2,1)S(1)} all-gather(bf16[64,128]{1,0:T(8,128)(2,1)S(1)} %multiply_convert_fusion), channel_id=1, replica_groups=mesh['row'=8,'col'=4] {'col'}, dimensions={1}, use_global_device_ids=true | all-gather | bytes 81920 | tf_op jit(solution)/shard_map/all_gather | solution.py:44
  160.5 0.1 reshape.171
  160.6 0.7 copy.49
  161.2 3.5 all-to-all-start.3
  164.8 1.0 gather_fusion.3
  165.8 3.9 %fusion.33 = bf16[64,152,128]{2,0,1:T(8,128)(2,1)S(1)} fusion(bf16[152,64,128]{2,1,0:T(8,128)(2,1)S(1)} %gather_fusion.3, bf16[1,1,152,128,128]{4,3,2,1,0:T(8,128)(2,1)} %param.6, pred[152]{0:T(512)(128)(4,1)S(1)} %compare_and_fusion), kind=kOutput, calls=%fused_computation.34 | convolution fusion | flops 321257472 | bytes 9961624 | tf_op jit(solution)/shard_map/sba,ksb->ksa/dot_general | solution.py:60
  169.7 1.4 fusion.45
  171.1 0.7 copy.55
  171.9 3.3 all-to-all-start.5
  175.2 0.0 reduce-scatter.12.cloned.1.call-start
  175.3 1.0 gather_fusion.2
  176.3 7.4 %fusion.30 = bf16[64,152,128]{2,0,1:T(8,128)(2,1)} fusion(bf16[152,64,128]{2,1,0:T(8,128)(2,1)S(1)} %gather_fusion.2, bf16[1,1,152,128,128]{4,3,2,1,0:T(8,128)(2,1)} %param.6, pred[152]{0:T(512)(128)(4,1)S(1)} %compare_and_fusion), kind=kOutput, calls=%fused_computation.33 | convolution fusion | flops 321257472 | bytes 9961624 | tf_op jit(solution)/shard_map/sab,ksb->ksa/dot_general | solution.py:55
  183.7 0.9 copy.72
  184.6 0.0 reduce-scatter.12.cloned.1.call-update
  184.6 3.1 fusion.63
  187.8 7.1 %all_to_all.46 = bf16[64,1,4,128]{3,0,1,2:T(8,128)(2,1)S(1)} all-to-all(bf16[64,1,4,128]{3,0,1,2:T(8,128)(2,1)S(1)} %copy.52), channel_id=1, replica_groups=mesh['row'=8,'col'=4] {'col'}, dimensions={2} | all-to-all | bytes 131072 | tf_op jit(solution)/shard_map/all_to_all | solution.py:68
  194.9 48.9 %reduce-scatter.12.cloned.1.call-done = bf16[128,64]{1,0:T(8,128)(2,1)} async-done(((bf16[1024,64]{1,0:T(8,128)(2,1)}), bf16[128,64]{1,0:T(8,128)(2,1)}) %reduce-scatter.12.cloned.1.call-update) | async-done | bytes 16400
  243.8 0.8 copy.68
  244.7 26.2 %all_gather.22 = bf16[64,1024]{1,0:T(8,128)(2,1)S(1)} all-gather(bf16[64,128]{1,0:T(8,128)(2,1)S(1)} %fusion.78), channel_id=1, replica_groups=mesh['row'=8,'col'=4] {'row'}, dimensions={1}, use_global_device_ids=true | all-gather | bytes 147456 | tf_op jit(solution)/shard_map/all_gather | solution.py:45
  270.9 5.3 %all_gather.23 = bf16[64,512]{1,0:T(8,128)(2,1)S(1)} all-gather(bf16[64,128]{1,0:T(8,128)(2,1)S(1)} %fusion.78), channel_id=1, replica_groups=mesh['row'=8,'col'=4] {'col'}, dimensions={1}, use_global_device_ids=true | all-gather | bytes 81920 | tf_op jit(solution)/shard_map/all_gather | solution.py:44
  276.1 0.1 reshape.176
  276.2 0.7 copy.57
  276.9 3.3 all-to-all-start.6
  280.2 1.0 gather_fusion.5
  281.3 3.9 %fusion.39 = bf16[64,152,128]{2,0,1:T(8,128)(2,1)S(1)} fusion(bf16[152,64,128]{2,1,0:T(8,128)(2,1)S(1)} %gather_fusion.5, bf16[1,1,152,128,128]{4,3,2,1,0:T(8,128)(2,1)} %param.6, pred[152]{0:T(512)(128)(4,1)S(1)} %compare_and_fusion), kind=kOutput, calls=%fused_computation.36 | convolution fusion | flops 321257472 | bytes 9961624 | tf_op jit(solution)/shard_map/sba,ksb->ksa/dot_general | solution.py:60
  285.2 1.4 fusion.48
  286.6 0.7 copy.63
  287.4 3.5 all-to-all-start.8
  290.9 0.0 reduce-scatter.14.cloned.1.call-start
  291.0 1.0 gather_fusion.4
  292.0 7.4 %fusion.36 = bf16[64,152,128]{2,0,1:T(8,128)(2,1)} fusion(bf16[152,64,128]{2,1,0:T(8,128)(2,1)S(1)} %gather_fusion.4, bf16[1,1,152,128,128]{4,3,2,1,0:T(8,128)(2,1)} %param.6, pred[152]{0:T(512)(128)(4,1)S(1)} %compare_and_fusion), kind=kOutput, calls=%fused_computation.35 | convolution fusion | flops 321257472 | bytes 9961624 | tf_op jit(solution)/shard_map/sab,ksb->ksa/dot_general | solution.py:55
  299.4 0.9 copy.73
  300.3 0.0 reduce-scatter.14.cloned.1.call-update
  300.3 3.1 fusion.60
  303.4 7.2 %all_to_all.47 = bf16[64,1,4,128]{3,0,1,2:T(8,128)(2,1)S(1)} all-to-all(bf16[64,1,4,128]{3,0,1,2:T(8,128)(2,1)S(1)} %copy.60), channel_id=1, replica_groups=mesh['row'=8,'col'=4] {'col'}, dimensions={2} | all-to-all | bytes 131072 | tf_op jit(solution)/shard_map/all_to_all | solution.py:68
  310.6 49.0 %reduce-scatter.14.cloned.1.call-done = bf16[128,64]{1,0:T(8,128)(2,1)} async-done(((bf16[1024,64]{1,0:T(8,128)(2,1)}), bf16[128,64]{1,0:T(8,128)(2,1)}) %reduce-scatter.14.cloned.1.call-update) | async-done | bytes 16400
  359.6 0.8 copy.70
  360.4 0.6 subtract_subtract_fusion
  (26 shorter events, 0.2 us)
Async XLA Ops:
  35.9 18.4 %all-to-all-start = ((bf16[64,2,4,128]{3,0,1,2:T(8,128)(2,1)}), bf16[64,2,4,128]{3,0,1,2:T(8,128)(2,1)S(1)}, u32[]{:S(2)}, u32[]{:S(2)}) async-start(bf16[64,2,4,128]{3,0,1,2:T(8,128)(2,1)} %copy.41), calls=%async_computation | async-start | bytes 262144 | tf_op jit(solution)/shard_map/all_to_all | solution.py:46
  47.1 1.1 copy-start.1
  47.1 1.1 copy-start.2
  54.3 11.8 %all-to-all-start.2 = ((bf16[64,2,4,128]{3,1,0,2:T(2,128)(2,1)}), bf16[64,2,4,128]{3,1,0,2:T(2,128)(2,1)S(1)}, u32[]{:S(2)}, u32[]{:S(2)}) async-start(bf16[64,2,4,128]{3,1,0,2:T(2,128)(2,1)} %copy.47), calls=%async_computation.2 | async-start | bytes 262144 | tf_op jit(solution)/shard_map/all_to_all | solution.py:69
  57.7 70.5 %reduce-scatter.10.cloned.1.call-start = ((), (), s32[]{:S(2)}) async-start(), calls=%async_computation.12 | async-start | bytes 294912
  66.2 62.9 %copy-start = (f32[64,128]{1,0:T(8,128)S(1)}, f32[64,128]{1,0:T(8,128)}, u32[]{:S(2)}) copy-start(f32[64,128]{1,0:T(8,128)} %param.5) | copy-start | bytes 98308
  161.2 10.7 %all-to-all-start.3 = ((bf16[64,2,4,128]{3,0,1,2:T(8,128)(2,1)}), bf16[64,2,4,128]{3,0,1,2:T(8,128)(2,1)S(1)}, u32[]{:S(2)}, u32[]{:S(2)}) async-start(bf16[64,2,4,128]{3,0,1,2:T(8,128)(2,1)} %copy.49), calls=%async_computation.3 | async-start | bytes 262144 | tf_op jit(solution)/shard_map/all_to_all | solution.py:46
  171.9 11.8 %all-to-all-start.5 = ((bf16[64,2,4,128]{3,1,0,2:T(2,128)(2,1)}), bf16[64,2,4,128]{3,1,0,2:T(2,128)(2,1)S(1)}, u32[]{:S(2)}, u32[]{:S(2)}) async-start(bf16[64,2,4,128]{3,1,0,2:T(2,128)(2,1)} %copy.55), calls=%async_computation.5 | async-start | bytes 262144 | tf_op jit(solution)/shard_map/all_to_all | solution.py:69
  175.2 68.6 %reduce-scatter.12.cloned.1.call-start = ((), (), s32[]{:S(2)}) async-start(), calls=%async_computation.13 | async-start | bytes 294912
  276.9 10.5 %all-to-all-start.6 = ((bf16[64,2,4,128]{3,0,1,2:T(8,128)(2,1)}), bf16[64,2,4,128]{3,0,1,2:T(8,128)(2,1)S(1)}, u32[]{:S(2)}, u32[]{:S(2)}) async-start(bf16[64,2,4,128]{3,0,1,2:T(8,128)(2,1)} %copy.57), calls=%async_computation.6 | async-start | bytes 262144 | tf_op jit(solution)/shard_map/all_to_all | solution.py:46
  287.4 12.1 %all-to-all-start.8 = ((bf16[64,2,4,128]{3,1,0,2:T(2,128)(2,1)}), bf16[64,2,4,128]{3,1,0,2:T(2,128)(2,1)S(1)}, u32[]{:S(2)}, u32[]{:S(2)}) async-start(bf16[64,2,4,128]{3,1,0,2:T(2,128)(2,1)} %copy.63), calls=%async_computation.8 | async-start | bytes 262144 | tf_op jit(solution)/shard_map/all_to_all | solution.py:69
  290.9 68.7 %reduce-scatter.14.cloned.1.call-start = ((), (), s32[]{:S(2)}) async-start(), calls=%async_computation.14 | async-start | bytes 294912
Sparse Core Ops, SparseCore 0:
  67.2 60.9 reduce-scatter.9
  184.7 59.0 reduce-scatter.11
  300.4 59.1 reduce-scatter.13
where the time goes:
time: 369 us; the launch traced here: 368 us
  waiting for transfers between devices  149 us (40%)
  blocking collectives  118 us (32%)
  matrix products  47.5 us (13%)
  starting transfers between devices  20.5 us (6%)
  local copies, waits for them, and re-layouts  15.9 us (4%)
  between operations  14.1 us (4%)
    unnamed x6, waiting for transfers between devices  149 us
    all_gather x3, blocking collectives, hamiltonian(): stacked = lax.all_gather(wire, 'row', axis=1, tiled=True)  80.2 us
    dot_general x3, matrix products, hamiltonian(): jnp.einsum('sab,ksb->ksa', values_live, inputs_col, preferred_element_typ...  22.2 us
    all_to_all x3, blocking collectives, hamiltonian(): lax.all_to_all(row_wire, 'col', split_axis=2, concat_axis=2, tiled=True)  21.4 us
    all_gather x3, blocking collectives, hamiltonian(): row_slab = lax.all_gather(wire, 'col', axis=1, tiled=True)  16.3 us
    dot_general x3, matrix products, hamiltonian(): jnp.einsum('sba,ksb->ksa', values_live, inputs_row, preferred_element_typ...  11.8 us
    all_to_all x3, starting transfers between devices, hamiltonian(): lax.all_to_all(col_wire, 'col', split_axis=2, concat_axis=2, tiled=True)  10.2 us
    all_to_all x3, starting transfers between devices, hamiltonian(): lax.all_to_all(stacked.reshape(width, slab_groups, col_count, piece_rows)...  10.1 us
  transfers between devices with their start and end apart: 9, of which 3 were waited for; matrix products, arithmetic and copies ran while one was open for 16% of the time, Pallas kernels for 0%

commit v1 on v0

v1 whole, which is shorter than its diff:
```python
import functools

import jax
import jax.numpy as jnp
from jax import lax
from jax.experimental import pallas as pl
from jax.experimental.pallas import tpu as pltpu
from jax.sharding import PartitionSpec as P

DEGREE = 3
CENTER = 0.25
HALF_WIDTH = 2.0
PARTS = 4
MESH = pl.DeviceIdType.MESH


def densify_kernel(
    row_count, col_count, chunks, rows_ref, cols_ref, count_ref, blocks_ref, dense_ref, buf, *rest
):
    accs, sems = rest[:-1], rest[-1]
    slots, size = buf.shape[0], buf.shape[1]
    per_chunk = slots // chunks
    groups = dense_ref.shape[0]
    slab = dense_ref.shape[1] // size
    positions = slab * groups * slab
    band = size // PARTS
    a, b = lax.axis_index("row"), lax.axis_index("col")
    count = count_ref[0, 0]

    def chunk_copy(k):
        span = pl.ds(k * per_chunk, per_chunk)
        return pltpu.make_async_copy(blocks_ref.at[0, 0, span], buf.at[span], sems.at[k])

    for k in range(chunks):
        chunk_copy(k).start()

    def clear(p, carry):
        for acc in accs:
            acc[p] = jnp.zeros(acc.shape[1:], acc.dtype)
        return carry

    lax.fori_loop(0, positions + 1, clear, 0)

    def add_slot(s):
        r = rows_ref[0, 0, s]
        c = cols_ref[0, 0, s]
        global_row = a * slab + r
        global_col = (b + col_count * lax.div(c, slab)) * slab + lax.rem(c, slab)
        live = (s < count) & (global_row <= global_col)
        p = jnp.where(live, r * (groups * slab) + c, positions)
        for q, acc in enumerate(accs):
            acc[p] += buf[s, q * band : (q + 1) * band, :].astype(jnp.float32)

    for k in range(chunks):
        chunk_copy(k).wait()

        def body(i, carry, k=k):
            add_slot(k * per_chunk + i)
            return carry

        lax.fori_loop(0, per_chunk, body, 0, unroll=True if slots % 19 == 0 and per_chunk <= 19 else 1)

    def store(n, carry):
        h, r = lax.div(n, slab), lax.rem(n, slab)
        for l in range(slab):
            p = r * (groups * slab) + h * slab + l
            for q, acc in enumerate(accs):
                start = pl.multiple_of(r * size + q * band, band)
                dense_ref[h, pl.ds(start, band), l * size : (l + 1) * size] = acc[p].astype(jnp.bfloat16)
        return carry

    lax.fori_loop(0, groups * slab, store, 0)


def filter_kernel(
    R, C, x_ref, dense_hbm, out_ref, dense, cur, prev, total, racc, wsend, xrow, xcol, rsend, csend,
    rterm, cterm, dsem, xr_s, xr_r, xc_s, xc_r, rt_s, rt_r, ct_s, ct_r,
):
    G = R // C
    width, piece = x_ref.shape
    slab = C * piece
    a, b = lax.axis_index("row"), lax.axis_index("col")
    my_group, my_col = a // C, a % C

    def alive(j):
        return j + C * (G - 1) >= a

    def above(h):
        return b + C * h > a

    live = alive(b)
    diag = my_col == b

    load = pltpu.make_async_copy(dense_hbm, dense, dsem)
    load.start()

    barrier = pltpu.get_barrier_semaphore()

    def greet(row, col):
        pl.semaphore_signal(barrier, inc=1, device_id=(row, col), device_id_type=MESH)

    for j in range(C):
        @pl.when(j != b)
        def _():
            greet(a, j)
    for i in range(R - 1):
        @pl.when(i < a)
        def _():
            greet(i, my_col)
    greeted = C - 1 + a
    for h in range(G):
        @pl.when(above(h))
        def _():
            for j in range(C):
                greet(b + C * h, j)
        greeted = greeted + jnp.where(above(h), C, 0)
    pl.semaphore_wait(barrier, greeted)

    def remote(src, dst, send, recv, row, col):
        return pltpu.make_async_remote_copy(
            src_ref=src, dst_ref=dst, send_sem=send, recv_sem=recv, device_id=(row, col), device_id_type=MESH
        )

    def send_x_col(t, i):
        return remote(wsend.at[t], xcol.at[t, my_group, b], xc_s.at[t, i], xc_r.at[t, my_group, b], i, my_col)

    def send_x_row(t, j):
        return remote(wsend.at[t], xrow.at[t, b], xr_s.at[t, j], xr_r.at[t, b], a, j)

    def send_col_term(t, h, j):
        return remote(csend.at[t, h, j], cterm.at[t, a], ct_s.at[t, h, j], ct_r.at[t, a], b + C * h, j)

    def send_row_term(t, j):
        return remote(rsend.at[t, j], rterm.at[t, b], rt_s.at[t, j], rt_r.at[t, b], a, j)

    def got_x_col(t, h, j):
        remote(wsend.at[t], xcol.at[t, h, j], xc_s.at[t, 0], xc_r.at[t, h, j], b + C * h, j).wait_recv()

    def got_x_row(t, j):
        remote(wsend.at[t], xrow.at[t, j], xr_s.at[t, j], xr_r.at[t, j], a, j).wait_recv()

    def got_col_term(t, i):
        remote(csend.at[t, 0, 0], cterm.at[t, i], ct_s.at[t, 0, 0], ct_r.at[t, i], i, my_col).wait_recv()

    def got_row_term(t, j):
        remote(rsend.at[t, j], rterm.at[t, j], rt_s.at[t, j], rt_r.at[t, j], a, j).wait_recv()

    def times(x, m):
        return lax.dot_general(x, m, (((1,), (0,)), ((), ())), preferred_element_type=jnp.float32)

    def times_t(x, m):
        return lax.dot_general(x, m, (((1,), (1,)), ((), ())), preferred_element_type=jnp.float32)

    cur[...] = x_ref[...]
    prev[...] = jnp.zeros_like(prev)

    def step(t, carry):
        w = cur[...].astype(jnp.bfloat16)
        wsend[t] = w
        for j in range(C):
            @pl.when((j != b) & alive(j))
            def _():
                send_x_row(t, j).start()
        for i in range(R - 1):
            @pl.when(i < a)
            def _():
                send_x_col(t, i).start()

        @pl.when(t == 0)
        def _():
            load.wait()

        @pl.when(live)
        def _():
            xrow[t, b] = w
            for j in range(C):
                @pl.when(j != b)
                def _():
                    got_x_row(t, j)
            xr = jnp.concatenate([xrow[t, j] for j in range(C)], axis=1)
            for h in range(G - 1, -1, -1):
                @pl.when(above(h))
                def _():
                    terms = times(xr, dense[h]).astype(jnp.bfloat16)
                    for j in range(C):
                        csend[t, h, j] = terms[:, j * piece : (j + 1) * piece]
                        send_col_term(t, h, j).start()

            @pl.when(diag)
            def _():
                racc[...] = times(xr, dense[my_group]) + times_t(xr, dense[my_group])

            @pl.when(jnp.logical_not(diag))
            def _():
                racc[...] = jnp.zeros_like(racc)

            for h in range(G):
                @pl.when(above(h))
                def _():
                    for j in range(C):
                        got_x_col(t, h, j)
                    xc = jnp.concatenate([xcol[t, h, j] for j in range(C)], axis=1)
                    racc[...] += times_t(xc, dense[h])

            for j in range(C):
                mine = racc[:, j * piece : (j + 1) * piece].astype(jnp.bfloat16)

                @pl.when(j != b)
                def _():
                    rsend[t, j] = mine
                    send_row_term(t, j).start()

                @pl.when(j == b)
                def _():
                    rterm[t, j] = mine

        total[...] = -CENTER * cur[...]
        for j in range(C):
            @pl.when(alive(j))
            def _():
                @pl.when(j != b)
                def _():
                    got_row_term(t, j)
                total[...] += rterm[t, j].astype(jnp.float32)
        for i in range(R - 1):
            @pl.when(i < a)
            def _():
                got_col_term(t, i)
                total[...] += cterm[t, i].astype(jnp.float32)
        scale = jnp.where(t == 0, 1.0 / HALF_WIDTH, 2.0 / HALF_WIDTH)
        following = scale * total[...] - prev[...]
        prev[...] = cur[...]
        cur[...] = following
        return carry

    lax.fori_loop(0, DEGREE, step, 0)
    out_ref[...] = cur[...]

    def drain(t, carry):
        for j in range(C):
            @pl.when((j != b) & alive(j))
            def _():
                send_x_row(t, j).wait_send()

            @pl.when((j != b) & live)
            def _():
                send_row_term(t, j).wait_send()
        for i in range(R - 1):
            @pl.when(i < a)
            def _():
                send_x_col(t, i).wait_send()
        for h in range(G):
            @pl.when(above(h))
            def _():
                for j in range(C):
                    send_col_term(t, h, j).wait_send()
        return carry

    lax.fori_loop(0, DEGREE, drain, 0)


def local(vectors, blocks, slot_block_rows, slot_block_columns, counts):
    width, piece = vectors.shape
    slots, size = blocks.shape[2], blocks.shape[3]
    R, C = lax.axis_size("row"), lax.axis_size("col")
    G = R // C
    slab = C * piece
    positions = (slab // size) ** 2 * G
    chunks = next(n for n in (8, 4, 2, 1) if slots % n == 0)
    bf16, f32 = jnp.bfloat16, jnp.float32
    smem, vmem = pl.BlockSpec(memory_space=pltpu.SMEM), pl.BlockSpec(memory_space=pltpu.VMEM)
    hbm = pl.BlockSpec(memory_space=pl.ANY)
    dense_shape = (G, slab, slab)
    dense = pl.pallas_call(
        functools.partial(densify_kernel, R, C, chunks),
        out_shape=jax.ShapeDtypeStruct(dense_shape, bf16),
        in_specs=[smem, smem, smem, hbm],
        out_specs=vmem,
        scratch_shapes=[pltpu.VMEM((slots, size, size), bf16)]
        + [pltpu.VMEM((positions + 1, size // PARTS, size), f32)] * PARTS
        + [pltpu.SemaphoreType.DMA((chunks,))],
        compiler_params=pltpu.CompilerParams(vmem_limit_bytes=60 * 2**20),
    )(slot_block_rows, slot_block_columns, counts, blocks)

    def dma(*shape):
        return pltpu.SemaphoreType.DMA((DEGREE,) + shape)

    def pieces(*shape):
        return pltpu.VMEM((DEGREE,) + shape + (width, piece), bf16)

    return pl.pallas_call(
        functools.partial(filter_kernel, R, C),
        out_shape=jax.ShapeDtypeStruct((width, piece), f32),
        in_specs=[vmem, hbm],
        out_specs=vmem,
        scratch_shapes=[
            pltpu.VMEM(dense_shape, bf16),
            pltpu.VMEM((width, piece), f32),
            pltpu.VMEM((width, piece), f32),
            pltpu.VMEM((width, piece), f32),
            pltpu.VMEM((width, slab), f32),
            pieces(),
            pieces(C),
            pieces(G, C),
            pieces(C),
            pieces(G, C),
            pieces(C),
            pieces(R),
            pltpu.SemaphoreType.DMA,
            dma(C),
            dma(C),
            dma(R),
            dma(G, C),
            dma(C),
            dma(C),
            dma(G, C),
            dma(R),
        ],
        compiler_params=pltpu.CompilerParams(
            collective_id=0, has_side_effects=True, vmem_limit_bytes=48 * 2**20
        ),
    )(vectors, dense)


def solution(mesh):
    in_specs = (
        P(None, ("row", "col")),
        P("row", "col", None, None, None),
        P("row", "col", None),
        P("row", "col", None),
        P("row", "col"),
    )
    out_specs = P(None, ("row", "col"))
    return jax.shard_map(local, mesh=mesh, in_specs=in_specs, out_specs=out_specs, check_vma=False)
```

time: 369 us -> 38.8 us (0.11)
  waiting for transfers between devices: 149 us -> 0 us
  blocking collectives: 118 us -> 0 us
  matrix products: 47.5 us -> 0 us
  Pallas kernels: 0 us -> 36.1 us
  starting transfers between devices: 20.5 us -> 0 us
  local copies, waits for them, and re-layouts: 15.9 us -> 1.84 us
  between operations: 14.1 us -> 0.69 us
    unnamed x6 -> x0, waiting for transfers between devices: 149 us -> none
    all_gather x6 -> x0, blocking collectives: 96.5 us -> none  [the longest x3 80.2 us: hamiltonian(): stacked = lax.all_gather(wire, 'row', axis=1, tiled=True)]
    dot_general x12 -> x0, matrix products: 47.5 us -> none  [the longest x3 22.2 us: hamiltonian(): jnp.einsum('sab,ksb->ksa', values_live, inputs_col, preferred_element_typ...]
    pallas_call x0 -> x2, Pallas kernels: none -> 36.1 us  [the longest x1 31.5 us: local(): pl.pallas_call(functools.partial(filter_kernel, R, C), out_shape=jax.Shap...]
    all_to_all x3 -> x0, blocking collectives: 21.4 us -> none  [hamiltonian(): lax.all_to_all(row_wire, 'col', split_axis=2, concat_axis=2, tiled=True)]
    all_to_all x6 -> x0, starting transfers between devices: 20.4 us -> none  [the longest x3 10.2 us: hamiltonian(): lax.all_to_all(col_wire, 'col', split_axis=2, concat_axis=2, tiled=True)]
    gather x6 -> x0, local copies, waits for them, and re-layouts: 6.21 us -> none  [the longest x3 3.1 us: hamiltonian(): row_slab.reshape(width, slab_blocks, block_size)[:, rows_here, :]]
    reshape x15 -> x0, local copies, waits for them, and re-layouts: 4.54 us -> none  [the longest x3 2.25 us: hamiltonian(): col_part.astype(jnp.bfloat16)]
  transfers between devices with their start and end apart: 9 -> 0, of which waited for: 3 -> 0; matrix products, arithmetic and copies ran while one was open for 16% -> 0% of each run, Pallas kernels for 0% -> 0%
where the time goes in v1:
time: 38.8 us; the launch traced here: 38.6 us
  Pallas kernels  36.1 us (93%)
  local copies, waits for them, and re-layouts  1.84 us (5%)
  between operations  0.69 us (2%)
    pallas_call x1, Pallas kernels, local(): pl.pallas_call(functools.partial(filter_kernel, R, C), out_shape=jax.Shap...  31.5 us
    pallas_call x1, Pallas kernels, local(): pl.pallas_call(functools.partial(densify_kernel, R, C, chunks), out_shape...  4.53 us
    unnamed x5, local copies, waits for them, and re-layouts  1.84 us

profile of v1, /device:TPU:0, one launch (start us, length us, event | category | flops | bytes accessed | tf_op | source)
XLA Modules:
  0.0 38.6 jit_solution(9114847990623562464)
XLA Ops:
  0.0 0.0 copy-start.1
  0.7 4.5 %shard_map.55.dense_hbm = bf16[2,512,512]{2,1,0:T(8,128)(2,1)} custom-call(s32[1,1,152]{2,1,0:T(1,128)} %rows_ref.1, s32[1,1,152]{2,1,0:T(1,128)} %cols_ref.1, s32[1,1]{1,0:T(1,128)S(6)} %copy.7.count_ref, bf16[1,1,152,128,128]{4,3,2,1,0:T(8,128)(2,1)} %blocks_ref.1), custom_call_target="tpu_custom_call" | custom-call | tf_op jit(solution)/shard_map/pallas_call | solution.py:274
  5.2 0.0 copy-done.1
  5.2 0.0 copy-start
  5.2 1.2 %copy-done = bf16[2,512,512]{2,1,0:T(8,128)(2,1)S(1)} copy-done((bf16[2,512,512]{2,1,0:T(8,128)(2,1)S(1)}, bf16[2,512,512]{2,1,0:T(8,128)(2,1)}, u32[]{:S(2)}) %copy-start) | copy-done | bytes 1048600
  6.4 31.5 %shard_map.56 = f32[64,128]{1,0:T(8,128)S(1)} custom-call(f32[64,128]{1,0:T(8,128)S(1)} %copy-done.1, bf16[2,512,512]{2,1,0:T(8,128)(2,1)S(1)} %copy-done), custom_call_target="tpu_custom_call" | custom-call | tf_op jit(solution)/shard_map/pallas_call | solution.py:291
  38.0 0.6 %copy.8 = f32[64,128]{1,0:T(8,128)} copy(f32[64,128]{1,0:T(8,128)S(1)} %shard_map.56) | data formatting | bytes 65536
Async XLA Ops:
  0.0 5.2 %copy-start.1 = (f32[64,128]{1,0:T(8,128)S(1)}, f32[64,128]{1,0:T(8,128)}, u32[]{:S(2)}) copy-start(f32[64,128]{1,0:T(8,128)} %x_ref.1) | copy-start | bytes 98308
  5.2 1.2 %copy-start = (bf16[2,512,512]{2,1,0:T(8,128)(2,1)S(1)}, bf16[2,512,512]{2,1,0:T(8,128)(2,1)}, u32[]{:S(2)}) copy-start(bf16[2,512,512]{2,1,0:T(8,128)(2,1)} %shard_map.55.dense_hbm) | copy-start | bytes 3145732

commit v2 on v1

v2 whole, which is shorter than its diff:
```python
import functools

import jax
import jax.numpy as jnp
from jax import lax
from jax.experimental import pallas as pl
from jax.experimental.pallas import tpu as pltpu
from jax.sharding import PartitionSpec as P

DEGREE = 3
CENTER = 0.25
HALF_WIDTH = 2.0
PARTS = 4
BATCHES = 2
MESH = pl.DeviceIdType.MESH


def densify_kernel(
    row_count, col_count, chunks, rows_ref, cols_ref, count_ref, blocks_ref, dense_ref, buf, *rest
):
    accs, sems = rest[:-1], rest[-1]
    slots, size = buf.shape[0], buf.shape[1]
    per_chunk = slots // chunks
    groups = dense_ref.shape[0]
    slab = dense_ref.shape[1] // size
    positions = slab * groups * slab
    band = size // PARTS
    a, b = lax.axis_index("row"), lax.axis_index("col")
    count = count_ref[0, 0]

    def chunk_copy(k):
        span = pl.ds(k * per_chunk, per_chunk)
        return pltpu.make_async_copy(blocks_ref.at[0, 0, span], buf.at[span], sems.at[k])

    for k in range(chunks):
        chunk_copy(k).start()

    def clear(p, carry):
        for acc in accs:
            acc[p] = jnp.zeros(acc.shape[1:], acc.dtype)
        return carry

    lax.fori_loop(0, positions + 1, clear, 0)

    def add_slot(s):
        r = rows_ref[0, 0, s]
        c = cols_ref[0, 0, s]
        global_row = a * slab + r
        global_col = (b + col_count * lax.div(c, slab)) * slab + lax.rem(c, slab)
        live = (s < count) & (global_row <= global_col)
        p = jnp.where(live, r * (groups * slab) + c, positions)
        for q, acc in enumerate(accs):
            acc[p] += buf[s, q * band : (q + 1) * band, :].astype(jnp.float32)

    for k in range(chunks):
        chunk_copy(k).wait()

        def body(i, carry, k=k):
            add_slot(k * per_chunk + i)
            return carry

        lax.fori_loop(0, per_chunk, body, 0, unroll=True if slots % 19 == 0 and per_chunk <= 19 else 1)

    def store(n, carry):
        h, r = lax.div(n, slab), lax.rem(n, slab)
        for l in range(slab):
            p = r * (groups * slab) + h * slab + l
            for q, acc in enumerate(accs):
                start = pl.multiple_of(r * size + q * band, band)
                dense_ref[h, pl.ds(start, band), l * size : (l + 1) * size] = acc[p].astype(jnp.bfloat16)
        return carry

    lax.fori_loop(0, groups * slab, store, 0)


def filter_kernel(
    R, C, x_ref, dense_hbm, out_ref, dense, cur, prev, total, racc, wsend, xrow, xcol, rsend, csend,
    rterm, cterm, dsem, xr_s, xr_r, xc_s, xc_r, rt_s, rt_r, ct_s, ct_r,
):
    G = R // C
    piece = x_ref.shape[1]
    V, rows = cur.shape[:2]
    a, b = lax.axis_index("row"), lax.axis_index("col")
    my_group, my_col = a // C, a % C

    def alive(j):
        return j + C * (G - 1) >= a

    def above(h):
        return b + C * h > a

    live = alive(b)
    diag = my_col == b

    load = pltpu.make_async_copy(dense_hbm, dense, dsem)
    load.start()

    barrier = pltpu.get_barrier_semaphore()

    def greet(row, col):
        pl.semaphore_signal(barrier, inc=1, device_id=(row, col), device_id_type=MESH)

    for j in range(C):
        @pl.when(j != b)
        def _():
            greet(a, j)
    for i in range(R - 1):
        @pl.when(i < a)
        def _():
            greet(i, my_col)
    greeted = C - 1 + a
    for h in range(G):
        @pl.when(above(h))
        def _():
            for j in range(C):
                greet(b + C * h, j)
        greeted = greeted + jnp.where(above(h), C, 0)
    pl.semaphore_wait(barrier, greeted)

    def remote(src, dst, send, recv, row, col):
        return pltpu.make_async_remote_copy(
            src_ref=src, dst_ref=dst, send_sem=send, recv_sem=recv, device_id=(row, col), device_id_type=MESH
        )

    def send_x_col(t, v, i):
        return remote(
            wsend.at[t, v], xcol.at[t, v, my_group, b], xc_s.at[t, v, i], xc_r.at[t, v, my_group, b], i, my_col
        )

    def send_x_row(t, v, j):
        return remote(wsend.at[t, v], xrow.at[t, v, b], xr_s.at[t, v, j], xr_r.at[t, v, b], a, j)

    def send_col_term(t, v, h, j):
        return remote(
            csend.at[t, v, h, j], cterm.at[t, v, a], ct_s.at[t, v, h, j], ct_r.at[t, v, a], b + C * h, j
        )

    def send_row_term(t, v, j):
        return remote(rsend.at[t, v, j], rterm.at[t, v, b], rt_s.at[t, v, j], rt_r.at[t, v, b], a, j)

    def got_x_col(t, v, h, j):
        remote(
            wsend.at[t, v], xcol.at[t, v, h, j], xc_s.at[t, v, 0], xc_r.at[t, v, h, j], b + C * h, j
        ).wait_recv()

    def got_x_row(t, v, j):
        remote(wsend.at[t, v], xrow.at[t, v, j], xr_s.at[t, v, j], xr_r.at[t, v, j], a, j).wait_recv()

    def got_col_term(t, v, i):
        remote(
            csend.at[t, v, 0, 0], cterm.at[t, v, i], ct_s.at[t, v, 0, 0], ct_r.at[t, v, i], i, my_col
        ).wait_recv()

    def got_row_term(t, v, j):
        remote(rsend.at[t, v, j], rterm.at[t, v, j], rt_s.at[t, v, j], rt_r.at[t, v, j], a, j).wait_recv()

    def times(x, m):
        return lax.dot_general(x, m, (((1,), (0,)), ((), ())), preferred_element_type=jnp.float32)

    def times_t(x, m):
        return lax.dot_general(x, m, (((1,), (1,)), ((), ())), preferred_element_type=jnp.float32)

    def side_by_side(ref, *index):
        return jnp.concatenate([ref[index + (j,)] for j in range(C)], axis=1)

    def hand_out(t, v):
        w = cur[v].astype(jnp.bfloat16)
        wsend[t, v] = w
        for j in range(C):
            @pl.when((j != b) & alive(j))
            def _():
                send_x_row(t, v, j).start()
        for i in range(R - 1):
            @pl.when(i < a)
            def _():
                send_x_col(t, v, i).start()

        @pl.when(live)
        def _():
            xrow[t, v, b] = w

    def column_terms(t, v):
        for j in range(C):
            @pl.when(j != b)
            def _():
                got_x_row(t, v, j)
        xr = side_by_side(xrow, t, v)
        for h in range(G - 1, -1, -1):
            @pl.when(above(h))
            def _():
                terms = times(xr, dense[h]).astype(jnp.bfloat16)
                for j in range(C):
                    csend[t, v, h, j] = terms[:, j * piece : (j + 1) * piece]
                    send_col_term(t, v, h, j).start()

    def diagonal_terms(t, v):
        @pl.when(diag)
        def _():
            xr = side_by_side(xrow, t, v)
            racc[v] = times(xr, dense[my_group]) + times_t(xr, dense[my_group])

        @pl.when(jnp.logical_not(diag))
        def _():
            racc[v] = jnp.zeros(racc.shape[1:], racc.dtype)

    def row_terms(t, v):
        for h in range(G):
            @pl.when(above(h))
            def _():
                for j in range(C):
                    got_x_col(t, v, h, j)
                racc[v] += times_t(side_by_side(xcol, t, v, h), dense[h])
        for j in range(C):
            mine = racc[v, :, j * piece : (j + 1) * piece].astype(jnp.bfloat16)

            @pl.when(j != b)
            def _():
                rsend[t, v, j] = mine
                send_row_term(t, v, j).start()

            @pl.when(j == b)
            def _():
                rterm[t, v, j] = mine

    def update(t, v):
        total[v] = -CENTER * cur[v]
        for j in range(C):
            @pl.when(alive(j))
            def _():
                @pl.when(j != b)
                def _():
                    got_row_term(t, v, j)
                total[v] += rterm[t, v, j].astype(jnp.float32)
        for i in range(R - 1):
            @pl.when(i < a)
            def _():
                got_col_term(t, v, i)
                total[v] += cterm[t, v, i].astype(jnp.float32)
        scale = jnp.where(t == 0, 1.0 / HALF_WIDTH, 2.0 / HALF_WIDTH)
        following = scale * total[v] - prev[v]
        prev[v] = cur[v]
        cur[v] = following

    for v in range(V):
        cur[v] = x_ref[v * rows : (v + 1) * rows, :]
        hand_out(0, v)
    prev[...] = jnp.zeros_like(prev)
    load.wait()

    def step(t, carry):
        @pl.when(live)
        def _():
            for v in range(V):
                column_terms(t, v)
            for v in range(V):
                diagonal_terms(t, v)
            for v in range(V):
                row_terms(t, v)
        for v in range(V):
            update(t, v)

            @pl.when(t < DEGREE - 1)
            def _():
                hand_out(t + 1, v)
        return carry

    lax.fori_loop(0, DEGREE, step, 0)
    for v in range(V):
        out_ref[v * rows : (v + 1) * rows, :] = cur[v]

    def drain(t, carry):
        for v in range(V):
            for j in range(C):
                @pl.when((j != b) & alive(j))
                def _():
                    send_x_row(t, v, j).wait_send()

                @pl.when((j != b) & live)
                def _():
                    send_row_term(t, v, j).wait_send()
            for i in range(R - 1):
                @pl.when(i < a)
                def _():
                    send_x_col(t, v, i).wait_send()
            for h in range(G):
                @pl.when(above(h))
                def _():
                    for j in range(C):
                        send_col_term(t, v, h, j).wait_send()
        return carry

    lax.fori_loop(0, DEGREE, drain, 0)


def local(vectors, blocks, slot_block_rows, slot_block_columns, counts):
    width, piece = vectors.shape
    slots, size = blocks.shape[2], blocks.shape[3]
    R, C = lax.axis_size("row"), lax.axis_size("col")
    G = R // C
    slab = C * piece
    rows = width // BATCHES
    positions = (slab // size) ** 2 * G
    chunks = next(n for n in (8, 4, 2, 1) if slots % n == 0)
    bf16, f32 = jnp.bfloat16, jnp.float32
    smem, vmem = pl.BlockSpec(memory_space=pltpu.SMEM), pl.BlockSpec(memory_space=pltpu.VMEM)
    hbm = pl.BlockSpec(memory_space=pl.ANY)
    dense_shape = (G, slab, slab)
    dense = pl.pallas_call(
        functools.partial(densify_kernel, R, C, chunks),
        out_shape=jax.ShapeDtypeStruct(dense_shape, bf16),
        in_specs=[smem, smem, smem, hbm],
        out_specs=vmem,
        scratch_shapes=[pltpu.VMEM((slots, size, size), bf16)]
        + [pltpu.VMEM((positions + 1, size // PARTS, size), f32)] * PARTS
        + [pltpu.SemaphoreType.DMA((chunks,))],
        compiler_params=pltpu.CompilerParams(vmem_limit_bytes=60 * 2**20),
    )(slot_block_rows, slot_block_columns, counts, blocks)

    def dma(*shape):
        return pltpu.SemaphoreType.DMA((DEGREE, BATCHES) + shape)

    def pieces(*shape):
        return pltpu.VMEM((DEGREE, BATCHES) + shape + (rows, piece), bf16)

    return pl.pallas_call(
        functools.partial(filter_kernel, R, C),
        out_shape=jax.ShapeDtypeStruct((width, piece), f32),
        in_specs=[vmem, hbm],
        out_specs=vmem,
        scratch_shapes=[
            pltpu.VMEM(dense_shape, bf16),
            pltpu.VMEM((BATCHES, rows, piece), f32),
            pltpu.VMEM((BATCHES, rows, piece), f32),
            pltpu.VMEM((BATCHES, rows, piece), f32),
            pltpu.VMEM((BATCHES, rows, slab), f32),
            pieces(),
            pieces(C),
            pieces(G, C),
            pieces(C),
            pieces(G, C),
            pieces(C),
            pieces(R),
            pltpu.SemaphoreType.DMA,
            dma(C),
            dma(C),
            dma(R),
            dma(G, C),
            dma(C),
            dma(C),
            dma(G, C),
            dma(R),
        ],
        compiler_params=pltpu.CompilerParams(
            collective_id=0, has_side_effects=True, vmem_limit_bytes=60 * 2**20
        ),
    )(vectors, dense)


def solution(mesh):
    in_specs = (
        P(None, ("row", "col")),
        P("row", "col", None, None, None),
        P("row", "col", None),
        P("row", "col", None),
        P("row", "col"),
    )
    out_specs = P(None, ("row", "col"))
    return jax.shard_map(local, mesh=mesh, in_specs=in_specs, out_specs=out_specs, check_vma=False)
```

time: 38.8 us -> 40.7 us (1.049)
  Pallas kernels: 36.1 us -> 38.4 us
  local copies, waits for them, and re-layouts: 1.84 us -> 1.38 us
    pallas_call x1, Pallas kernels: 31.5 us -> 33.8 us  [local(): pl.pallas_call(functools.partial(filter_kernel, R, C), out_shape=jax.Shap...]
    unnamed x5 -> x1, local copies, waits for them, and re-layouts: 1.84 us -> 1.38 us
where the time goes in v2:
time: 40.7 us; the launch traced here: 40.4 us
  Pallas kernels  38.4 us (94%)
  local copies, waits for them, and re-layouts  1.38 us (3%)
  between operations  0.67 us (2%)
    pallas_call x1, Pallas kernels, local(): pl.pallas_call(functools.partial(filter_kernel, R, C), out_shape=jax.Shap...  33.8 us
    pallas_call x1, Pallas kernels, local(): pl.pallas_call(functools.partial(densify_kernel, R, C, chunks), out_shape...  4.54 us
    unnamed x1, local copies, waits for them, and re-layouts  1.38 us

profile of v2, /device:TPU:0, one launch (start us, length us, event | category | flops | bytes accessed | tf_op | source)
XLA Modules:
  0.0 40.4 jit_solution(14581061992361111335)
XLA Ops:
  0.7 4.5 %shard_map.55.dense_hbm = bf16[2,512,512]{2,1,0:T(8,128)(2,1)} custom-call(s32[1,1,152]{2,1,0:T(1,128)} %rows_ref.1, s32[1,1,152]{2,1,0:T(1,128)} %cols_ref.1, s32[1,1]{1,0:T(1,128)S(6)} %copy.7.count_ref, bf16[1,1,152,128,128]{4,3,2,1,0:T(8,128)(2,1)} %blocks_ref.1), custom_call_target="tpu_custom_call" | custom-call | tf_op jit(solution)/shard_map/pallas_call | solution.py:308
  5.2 33.8 %shard_map.56 = f32[64,128]{1,0:T(8,128)} custom-call(f32[64,128]{1,0:T(8,128)} %x_ref.1, bf16[2,512,512]{2,1,0:T(8,128)(2,1)} %shard_map.55.dense_hbm), custom_call_target="tpu_custom_call" | custom-call | tf_op jit(solution)/shard_map/pallas_call | solution.py:325
  39.0 1.4 %copy.8 = f32[64,128]{1,0:T(8,128)} copy(f32[64,128]{1,0:T(8,128)} %shard_map.56) | data formatting | bytes 65536

commit v3 on v2

--- a/solution.py
+++ b/solution.py
@@ -11,7 +11,8 @@
 CENTER = 0.25
 HALF_WIDTH = 2.0
 PARTS = 4
-BATCHES = 2
+BATCHES = 1
+TILE = 256
 MESH = pl.DeviceIdType.MESH
 
 
@@ -74,8 +75,8 @@
 
 
 def filter_kernel(
-    R, C, x_ref, dense_hbm, out_ref, dense, cur, prev, total, racc, wsend, xrow, xcol, rsend, csend,
-    rterm, cterm, dsem, xr_s, xr_r, xc_s, xc_r, rt_s, rt_r, ct_s, ct_r,
+    R, C, x_ref, dense, out_ref, dense_t, cur, prev, total, racc, wsend, xrow, xcol, rsend, csend,
+    rterm, cterm, xr_s, xr_r, xc_s, xc_r, rt_s, rt_r, ct_s, ct_r,
 ):
     G = R // C
     piece = x_ref.shape[1]
@@ -92,9 +93,6 @@
     live = alive(b)
     diag = my_col == b
 
-    load = pltpu.make_async_copy(dense_hbm, dense, dsem)
-    load.start()
-
     barrier = pltpu.get_barrier_semaphore()
 
     def greet(row, col):
@@ -157,8 +155,16 @@
     def times(x, m):
         return lax.dot_general(x, m, (((1,), (0,)), ((), ())), preferred_element_type=jnp.float32)
 
-    def times_t(x, m):
-        return lax.dot_general(x, m, (((1,), (1,)), ((), ())), preferred_element_type=jnp.float32)
+    def transpose_dense():
+        n = dense.shape[1] // TILE
+
+        def tile(k, carry):
+            h, i, j = k // (n * n), (k // n) % n, k % n
+            down, across = pl.ds(pl.multiple_of(i * TILE, TILE), TILE), pl.ds(pl.multiple_of(j * TILE, TILE), TILE)
+            dense_t[h, across, down] = dense[h, down, across].T
+            return carry
+
+        lax.fori_loop(0, G * n * n, tile, 0)
 
     def side_by_side(ref, *index):
         return jnp.concatenate([ref[index + (j,)] for j in range(C)], axis=1)
@@ -197,7 +203,7 @@
         @pl.when(diag)
         def _():
             xr = side_by_side(xrow, t, v)
-            racc[v] = times(xr, dense[my_group]) + times_t(xr, dense[my_group])
+            racc[v] = times(xr, dense[my_group]) + times(xr, dense_t[my_group])
 
         @pl.when(jnp.logical_not(diag))
         def _():
@@ -209,7 +215,7 @@
             def _():
                 for j in range(C):
                     got_x_col(t, v, h, j)
-                racc[v] += times_t(side_by_side(xcol, t, v, h), dense[h])
+                racc[v] += times(side_by_side(xcol, t, v, h), dense_t[h])
         for j in range(C):
             mine = racc[v, :, j * piece : (j + 1) * piece].astype(jnp.bfloat16)
 
@@ -245,39 +251,13 @@
         cur[v] = x_ref[v * rows : (v + 1) * rows, :]
         hand_out(0, v)
     prev[...] = jnp.zeros_like(prev)
-    load.wait()
-
-    def step(t, carry):
-        @pl.when(live)
-        def _():
-            for v in range(V):
-                column_terms(t, v)
-            for v in range(V):
-                diagonal_terms(t, v)
-            for v in range(V):
-                row_terms(t, v)
-        for v in range(V):
-            update(t, v)
-
-            @pl.when(t < DEGREE - 1)
-            def _():
-                hand_out(t + 1, v)
-        return carry
-
-    lax.fori_loop(0, DEGREE, step, 0)
-    for v in range(V):
-        out_ref[v * rows : (v + 1) * rows, :] = cur[v]
-
-    def drain(t, carry):
+
+    def sent_early(t):
         for v in range(V):
             for j in range(C):
                 @pl.when((j != b) & alive(j))
                 def _():
                     send_x_row(t, v, j).wait_send()
-
-                @pl.when((j != b) & live)
-                def _():
-                    send_row_term(t, v, j).wait_send()
             for i in range(R - 1):
                 @pl.when(i < a)
                 def _():
@@ -287,9 +267,52 @@
                 def _():
                     for j in range(C):
                         send_col_term(t, v, h, j).wait_send()
+
+    def sent_late(t):
+        @pl.when(live)
+        def _():
+            for v in range(V):
+                for j in range(C):
+                    @pl.when(j != b)
+                    def _():
+                        send_row_term(t, v, j).wait_send()
+
+    def step(t, carry):
+        @pl.when(live)
+        def _():
+            for v in range(V):
+                column_terms(t, v)
+
+            @pl.when(t == 0)
+            def _():
+                transpose_dense()
+
+            for v in range(V):
+                diagonal_terms(t, v)
+            for v in range(V):
+                row_terms(t, v)
+        sent_early(t)
+
+        @pl.when(t > 0)
+        def _():
+            sent_late(t - 1)
+
+        for v in range(V):
+            update(t, v)
+
+            @pl.when(t < DEGREE - 1)
+            def _():
+                hand_out(t + 1, v)
         return carry
 
-    lax.fori_loop(0, DEGREE, drain, 0)
+    lax.fori_loop(0, DEGREE, step, 0)
+    for v in range(V):
+        out_ref[v * rows : (v + 1) * rows, :] = cur[v]
+    sent_late(DEGREE - 1)
+
+
+def vmem_limit(least, *sizes):
+    return int(min(60 * 2**20, max(least, sum(sizes) + 4 * 2**20)))
 
 
 def local(vectors, blocks, slot_block_rows, slot_block_columns, counts):
@@ -303,7 +326,7 @@
     chunks = next(n for n in (8, 4, 2, 1) if slots % n == 0)
     bf16, f32 = jnp.bfloat16, jnp.float32
     smem, vmem = pl.BlockSpec(memory_space=pltpu.SMEM), pl.BlockSpec(memory_space=pltpu.VMEM)
-    hbm = pl.BlockSpec(memory_space=pl.ANY)
+    hbm = pl.BlockSpec(memory_space=pltpu.HBM)
     dense_shape = (G, slab, slab)
     dense = pl.pallas_call(
         functools.partial(densify_kernel, R, C, chunks),
@@ -313,7 +336,7 @@
         scratch_shapes=[pltpu.VMEM((slots, size, size), bf16)]
         + [pltpu.VMEM((positions + 1, size // PARTS, size), f32)] * PARTS
         + [pltpu.SemaphoreType.DMA((chunks,))],
-        compiler_params=pltpu.CompilerParams(vmem_limit_bytes=60 * 2**20),
+        compiler_params=pltpu.CompilerParams(vmem_limit_bytes=vmem_limit(51 * 2**20, 2 * slots * size**2, 4 * positions * size**2, 2 * G * slab**2)),
     )(slot_block_rows, slot_block_columns, counts, blocks)
 
     def dma(*shape):
@@ -325,7 +348,7 @@
     return pl.pallas_call(
         functools.partial(filter_kernel, R, C),
         out_shape=jax.ShapeDtypeStruct((width, piece), f32),
-        in_specs=[vmem, hbm],
+        in_specs=[vmem, vmem],
         out_specs=vmem,
         scratch_shapes=[
             pltpu.VMEM(dense_shape, bf16),
@@ -340,7 +363,6 @@
             pieces(G, C),
             pieces(C),
             pieces(R),
-            pltpu.SemaphoreType.DMA,
             dma(C),
             dma(C),
             dma(R),
@@ -351,7 +373,7 @@
             dma(R),
         ],
         compiler_params=pltpu.CompilerParams(
-            collective_id=0, has_side_effects=True, vmem_limit_bytes=60 * 2**20
+            collective_id=0, has_side_effects=True, vmem_limit_bytes=vmem_limit(16 * 2**20, 4 * G * slab**2, 12 * DEGREE * (R + C) * width * piece)
         ),
     )(vectors, dense)
 

time: 40.7 us -> 37.9 us (0.931)
  Pallas kernels: 38.4 us -> 35 us
  local copies, waits for them, and re-layouts: 1.38 us -> 1.97 us
    pallas_call x1, Pallas kernels: 33.8 us -> 31.6 us  [local(): pl.pallas_call(functools.partial(filter_kernel, R, C), out_shape=jax.Shap...]
    pallas_call x1, Pallas kernels: 4.54 us -> 3.4 us  [local(): pl.pallas_call(functools.partial(densify_kernel, R, C, chunks), out_shape...]
    unnamed x1 -> x7, local copies, waits for them, and re-layouts: 1.38 us -> 1.97 us
where the time goes in v3:
time: 37.9 us; the launch traced here: 37.7 us
  Pallas kernels  35 us (92%)
  local copies, waits for them, and re-layouts  1.97 us (5%)
  between operations  0.69 us (2%)
    pallas_call x1, Pallas kernels, local(): pl.pallas_call(functools.partial(filter_kernel, R, C), out_shape=jax.Shap...  31.6 us
    pallas_call x1, Pallas kernels, local(): pl.pallas_call(functools.partial(densify_kernel, R, C, chunks), out_shape...  3.4 us
    unnamed x7, local copies, waits for them, and re-layouts  1.97 us

profile of v3, /device:TPU:0, one launch (start us, length us, event | category | flops | bytes accessed | tf_op | source)
XLA Modules:
  0.0 37.7 jit_solution(1211054548405656562)
XLA Ops:
  0.0 0.0 copy-start
  0.7 0.0 copy-start.1
  0.7 0.7 %copy-done.1 = s32[1,1,152]{2,1,0:T(1,128)S(1)} copy-done((s32[1,1,152]{2,1,0:T(1,128)S(1)}, s32[1,1,152]{2,1,0:T(1,128)}, u32[]{:S(2)}) %copy-start.1) | copy-done | bytes 632
  1.3 0.0 copy-start.2
  1.3 0.7 %copy-done.2 = s32[1,1,152]{2,1,0:T(1,128)S(1)} copy-done((s32[1,1,152]{2,1,0:T(1,128)S(1)}, s32[1,1,152]{2,1,0:T(1,128)}, u32[]{:S(2)}) %copy-start.2) | copy-done | bytes 632
  2.0 3.4 %shard_map.55.dense = bf16[2,512,512]{2,1,0:T(8,128)(2,1)S(1)} custom-call(s32[1,1,152]{2,1,0:T(1,128)S(1)} %copy-done.1, s32[1,1,152]{2,1,0:T(1,128)S(1)} %copy-done.2, s32[1,1]{1,0:T(1,128)S(6)} %copy.7.count_ref, bf16[1,1,152,128,128]{4,3,2,1,0:T(8,128)(2,1)} %blocks_ref.1), custom_call_target="tpu_custom_call" | custom-call | tf_op jit(solution)/shard_map/pallas_call | solution.py:331
  5.4 0.0 copy-done
  5.4 31.6 %shard_map.56 = f32[64,128]{1,0:T(8,128)S(1)} custom-call(f32[64,128]{1,0:T(8,128)S(1)} %copy-done, bf16[2,512,512]{2,1,0:T(8,128)(2,1)S(1)} %shard_map.55.dense), custom_call_target="tpu_custom_call" | custom-call | tf_op jit(solution)/shard_map/pallas_call | solution.py:348
  37.1 0.6 %copy.8 = f32[64,128]{1,0:T(8,128)} copy(f32[64,128]{1,0:T(8,128)S(1)} %shard_map.56) | data formatting | bytes 65536
Async XLA Ops:
  0.0 5.4 %copy-start = (f32[64,128]{1,0:T(8,128)S(1)}, f32[64,128]{1,0:T(8,128)}, u32[]{:S(2)}) copy-start(f32[64,128]{1,0:T(8,128)} %x_ref.1) | copy-start | bytes 98308
  0.7 0.7 %copy-start.1 = (s32[1,1,152]{2,1,0:T(1,128)S(1)}, s32[1,1,152]{2,1,0:T(1,128)}, u32[]{:S(2)}) copy-start(s32[1,1,152]{2,1,0:T(1,128)} %rows_ref.1) | copy-start | bytes 1828
  1.3 0.7 %copy-start.2 = (s32[1,1,152]{2,1,0:T(1,128)S(1)}, s32[1,1,152]{2,1,0:T(1,128)}, u32[]{:S(2)}) copy-start(s32[1,1,152]{2,1,0:T(1,128)} %cols_ref.1) | copy-start | bytes 1828

commit v4 on v3

--- a/solution.py
+++ b/solution.py
@@ -12,71 +12,13 @@
 HALF_WIDTH = 2.0
 PARTS = 4
 BATCHES = 1
-TILE = 256
 MESH = pl.DeviceIdType.MESH
 
 
-def densify_kernel(
-    row_count, col_count, chunks, rows_ref, cols_ref, count_ref, blocks_ref, dense_ref, buf, *rest
-):
-    accs, sems = rest[:-1], rest[-1]
-    slots, size = buf.shape[0], buf.shape[1]
-    per_chunk = slots // chunks
-    groups = dense_ref.shape[0]
-    slab = dense_ref.shape[1] // size
-    positions = slab * groups * slab
-    band = size // PARTS
-    a, b = lax.axis_index("row"), lax.axis_index("col")
-    count = count_ref[0, 0]
-
-    def chunk_copy(k):
-        span = pl.ds(k * per_chunk, per_chunk)
-        return pltpu.make_async_copy(blocks_ref.at[0, 0, span], buf.at[span], sems.at[k])
-
-    for k in range(chunks):
-        chunk_copy(k).start()
-
-    def clear(p, carry):
-        for acc in accs:
-            acc[p] = jnp.zeros(acc.shape[1:], acc.dtype)
-        return carry
-
-    lax.fori_loop(0, positions + 1, clear, 0)
-
-    def add_slot(s):
-        r = rows_ref[0, 0, s]
-        c = cols_ref[0, 0, s]
-        global_row = a * slab + r
-        global_col = (b + col_count * lax.div(c, slab)) * slab + lax.rem(c, slab)
-        live = (s < count) & (global_row <= global_col)
-        p = jnp.where(live, r * (groups * slab) + c, positions)
-        for q, acc in enumerate(accs):
-            acc[p] += buf[s, q * band : (q + 1) * band, :].astype(jnp.float32)
-
-    for k in range(chunks):
-        chunk_copy(k).wait()
-
-        def body(i, carry, k=k):
-            add_slot(k * per_chunk + i)
-            return carry
-
-        lax.fori_loop(0, per_chunk, body, 0, unroll=True if slots % 19 == 0 and per_chunk <= 19 else 1)
-
-    def store(n, carry):
-        h, r = lax.div(n, slab), lax.rem(n, slab)
-        for l in range(slab):
-            p = r * (groups * slab) + h * slab + l
-            for q, acc in enumerate(accs):
-                start = pl.multiple_of(r * size + q * band, band)
-                dense_ref[h, pl.ds(start, band), l * size : (l + 1) * size] = acc[p].astype(jnp.bfloat16)
-        return carry
-
-    lax.fori_loop(0, groups * slab, store, 0)
-
-
 def filter_kernel(
-    R, C, x_ref, dense, out_ref, dense_t, cur, prev, total, racc, wsend, xrow, xcol, rsend, csend,
+    R, C, chunks, x_ref, rows_ref, cols_ref, count_ref, blocks_ref, out_ref, dense, cur, prev, total, racc, wsend, xrow, xcol, rsend, csend,
     rterm, cterm, xr_s, xr_r, xc_s, xc_r, rt_s, rt_r, ct_s, ct_r,
+    rows_v, cols_v, in_s, buf, block_s, before_v, last_v, before_ref, last_ref, chain_s, *sums,
 ):
     G = R // C
     piece = x_ref.shape[1]
@@ -93,6 +35,60 @@
     live = alive(b)
     diag = my_col == b
 
+    slots, size = buf.shape[:2]
+    per_chunk, slab_blocks, band = slots // chunks, dense.shape[1] // size, size // PARTS
+
+    def chunk_copy(k):
+        span = pl.ds(k * per_chunk, per_chunk)
+        return pltpu.make_async_copy(blocks_ref.at[0, 0, span], buf.at[span], block_s.at[k])
+
+    def slot_copies():
+        return (
+            pltpu.make_async_copy(rows_ref, rows_v, in_s.at[0]),
+            pltpu.make_async_copy(cols_ref, cols_v, in_s.at[1]),
+        )
+
+    def vector_copy(v):
+        return pltpu.make_async_copy(x_ref.at[pl.ds(v * rows, rows)], cur.at[v], in_s.at[2 + v])
+
+    @pl.when(live)
+    def _():
+        for copy in slot_copies():
+            copy.start()
+
+    for v in range(V):
+        vector_copy(v).start()
+
+    @pl.when(live)
+    def _():
+        for k in range(chunks):
+            chunk_copy(k).start()
+
+    def link_slots():
+        positions = last_v.shape[1]
+        r, c = rows_v[0], cols_v[0]
+        ids = lax.broadcasted_iota(jnp.int32, (1, slots), 1)
+        global_row = a * slab_blocks + r
+        global_col = (b + C * lax.div(c, slab_blocks)) * slab_blocks + lax.rem(c, slab_blocks)
+        used = (ids < count_ref[0, 0]) & (global_row <= global_col)
+        key = jnp.where(used, r * (G * slab_blocks) + c, positions)
+        down = lax.broadcasted_iota(jnp.int32, (slots, slots), 0)
+        across = lax.broadcasted_iota(jnp.int32, (slots, slots), 1)
+        keys = jnp.broadcast_to(key, (slots, slots))
+        column = jnp.max(jnp.where(down == across, keys, 0), axis=1, keepdims=True)
+        before_v[...] = jnp.max(
+            jnp.where((column == keys) & (down < across), down + 1, 0), axis=0, keepdims=True
+        )
+        place = lax.broadcasted_iota(jnp.int32, (slots, positions), 1)
+        order = lax.broadcasted_iota(jnp.int32, (slots, positions), 0)
+        last_v[...] = jnp.max(jnp.where(column == place, order + 1, 0), axis=0, keepdims=True)
+
+    def chain_copies():
+        return (
+            pltpu.make_async_copy(before_v, before_ref, chain_s.at[0]),
+            pltpu.make_async_copy(last_v, last_ref, chain_s.at[1]),
+        )
+
     barrier = pltpu.get_barrier_semaphore()
 
     def greet(row, col):
@@ -113,6 +109,15 @@
             for j in range(C):
                 greet(b + C * h, j)
         greeted = greeted + jnp.where(above(h), C, 0)
+
+    @pl.when(live)
+    def _():
+        for copy in slot_copies():
+            copy.wait()
+        link_slots()
+        for copy in chain_copies():
+            copy.start()
+
     pl.semaphore_wait(barrier, greeted)
 
     def remote(src, dst, send, recv, row, col):
@@ -155,16 +160,36 @@
     def times(x, m):
         return lax.dot_general(x, m, (((1,), (0,)), ((), ())), preferred_element_type=jnp.float32)
 
-    def transpose_dense():
-        n = dense.shape[1] // TILE
-
-        def tile(k, carry):
-            h, i, j = k // (n * n), (k // n) % n, k % n
-            down, across = pl.ds(pl.multiple_of(i * TILE, TILE), TILE), pl.ds(pl.multiple_of(j * TILE, TILE), TILE)
-            dense_t[h, across, down] = dense[h, down, across].T
+    def times_t(x, m):
+        return lax.dot_general(x, m, (((1,), (1,)), ((), ())), preferred_element_type=jnp.float32)
+
+    def densify():
+        for copy in chain_copies():
+            copy.wait()
+        for part in sums:
+            part[0] = jnp.zeros(part.shape[1:], part.dtype)
+
+        def chunk(k, carry):
+            chunk_copy(k).wait()
+            for n in range(per_chunk):
+                s = k * per_chunk + n
+                before = before_ref[0, s]
+                for q, part in enumerate(sums):
+                    part[s + 1] = part[before] + buf[s, q * band : (q + 1) * band, :].astype(jnp.float32)
             return carry
 
-        lax.fori_loop(0, G * n * n, tile, 0)
+        lax.fori_loop(0, chunks, chunk, 0)
+
+        def store(n, carry):
+            h, r = n // slab_blocks, n % slab_blocks
+            for l in range(slab_blocks):
+                last = last_ref[0, (r * G + h) * slab_blocks + l]
+                for q, part in enumerate(sums):
+                    start = pl.multiple_of(r * size + q * band, band)
+                    dense[h, pl.ds(start, band), l * size : (l + 1) * size] = part[last].astype(jnp.bfloat16)
+            return carry
+
+        lax.fori_loop(0, G * slab_blocks, store, 0)
 
     def side_by_side(ref, *index):
         return jnp.concatenate([ref[index + (j,)] for j in range(C)], axis=1)
@@ -203,7 +228,7 @@
         @pl.when(diag)
         def _():
             xr = side_by_side(xrow, t, v)
-            racc[v] = times(xr, dense[my_group]) + times(xr, dense_t[my_group])
+            racc[v] = times(xr, dense[my_group]) + times_t(xr, dense[my_group])
 
         @pl.when(jnp.logical_not(diag))
         def _():
@@ -215,7 +240,7 @@
             def _():
                 for j in range(C):
                     got_x_col(t, v, h, j)
-                racc[v] += times(side_by_side(xcol, t, v, h), dense_t[h])
+                racc[v] += times_t(side_by_side(xcol, t, v, h), dense[h])
         for j in range(C):
             mine = racc[v, :, j * piece : (j + 1) * piece].astype(jnp.bfloat16)
 
@@ -248,9 +273,13 @@
         cur[v] = following
 
     for v in range(V):
-        cur[v] = x_ref[v * rows : (v + 1) * rows, :]
+        vector_copy(v).wait()
         hand_out(0, v)
     prev[...] = jnp.zeros_like(prev)
+
+    @pl.when(live)
+    def _():
+        densify()
 
     def sent_early(t):
         for v in range(V):
@@ -283,10 +312,6 @@
             for v in range(V):
                 column_terms(t, v)
 
-            @pl.when(t == 0)
-            def _():
-                transpose_dense()
-
             for v in range(V):
                 diagonal_terms(t, v)
             for v in range(V):
@@ -327,17 +352,6 @@
     bf16, f32 = jnp.bfloat16, jnp.float32
     smem, vmem = pl.BlockSpec(memory_space=pltpu.SMEM), pl.BlockSpec(memory_space=pltpu.VMEM)
     hbm = pl.BlockSpec(memory_space=pltpu.HBM)
-    dense_shape = (G, slab, slab)
-    dense = pl.pallas_call(
-        functools.partial(densify_kernel, R, C, chunks),
-        out_shape=jax.ShapeDtypeStruct(dense_shape, bf16),
-        in_specs=[smem, smem, smem, hbm],
-        out_specs=vmem,
-        scratch_shapes=[pltpu.VMEM((slots, size, size), bf16)]
-        + [pltpu.VMEM((positions + 1, size // PARTS, size), f32)] * PARTS
-        + [pltpu.SemaphoreType.DMA((chunks,))],
-        compiler_params=pltpu.CompilerParams(vmem_limit_bytes=vmem_limit(51 * 2**20, 2 * slots * size**2, 4 * positions * size**2, 2 * G * slab**2)),
-    )(slot_block_rows, slot_block_columns, counts, blocks)
 
     def dma(*shape):
         return pltpu.SemaphoreType.DMA((DEGREE, BATCHES) + shape)
@@ -346,12 +360,12 @@
         return pltpu.VMEM((DEGREE, BATCHES) + shape + (rows, piece), bf16)
 
     return pl.pallas_call(
-        functools.partial(filter_kernel, R, C),
+        functools.partial(filter_kernel, R, C, chunks),
         out_shape=jax.ShapeDtypeStruct((width, piece), f32),
-        in_specs=[vmem, vmem],
+        in_specs=[hbm, hbm, hbm, smem, hbm],
         out_specs=vmem,
         scratch_shapes=[
-            pltpu.VMEM(dense_shape, bf16),
+            pltpu.VMEM((G, slab, slab), bf16),
             pltpu.VMEM((BATCHES, rows, piece), f32),
             pltpu.VMEM((BATCHES, rows, piece), f32),
             pltpu.VMEM((BATCHES, rows, piece), f32),
@@ -371,11 +385,22 @@
             dma(C),
             dma(G, C),
             dma(R),
-        ],
+            pltpu.VMEM((1, 1, slots), jnp.int32),
+            pltpu.VMEM((1, 1, slots), jnp.int32),
+            pltpu.SemaphoreType.DMA((2 + BATCHES,)),
+            pltpu.VMEM((slots, size, size), bf16),
+            pltpu.SemaphoreType.DMA((chunks,)),
+            pltpu.VMEM((1, slots), jnp.int32),
+            pltpu.VMEM((1, positions), jnp.int32),
+            pltpu.SMEM((1, slots), jnp.int32),
+            pltpu.SMEM((1, positions), jnp.int32),
+            pltpu.SemaphoreType.DMA((2,)),
+        ]
+        + [pltpu.VMEM((slots + 1, size // PARTS, size), f32)] * PARTS,
         compiler_params=pltpu.CompilerParams(
-            collective_id=0, has_side_effects=True, vmem_limit_bytes=vmem_limit(16 * 2**20, 4 * G * slab**2, 12 * DEGREE * (R + C) * width * piece)
+            collective_id=0, has_side_effects=True, vmem_limit_bytes=vmem_limit(60 * 2**20, 6 * slots * size**2, 2 * G * slab**2, 12 * DEGREE * (R + C) * width * piece)
         ),
-    )(vectors, dense)
+    )(vectors, slot_block_rows, slot_block_columns, counts, blocks)
 
 
 def solution(mesh):

time: 37.9 us -> 34.5 us (0.910)
  Pallas kernels: 35 us -> 32.2 us
  local copies, waits for them, and re-layouts: 1.97 us -> 1.38 us
    pallas_call x2 -> x1, Pallas kernels: 35 us -> 32.2 us  [local(): pl.pallas_call(functools.partial(filter_kernel, R, C, chunks), out_shape=...]
    unnamed x7 -> x1, local copies, waits for them, and re-layouts: 1.97 us -> 1.38 us
where the time goes in v4:
time: 34.5 us; the launch traced here: 34.3 us
  Pallas kernels  32.2 us (93%)
  local copies, waits for them, and re-layouts  1.38 us (4%)
  between operations  0.66 us (2%)
    pallas_call x1, Pallas kernels, local(): pl.pallas_call(functools.partial(filter_kernel, R, C, chunks), out_shape=...  32.2 us
    unnamed x1, local copies, waits for them, and re-layouts  1.38 us

profile of v4, /device:TPU:0, one launch (start us, length us, event | category | flops | bytes accessed | tf_op | source)
XLA Modules:
  0.0 34.3 jit_solution(16947476860070990988)
XLA Ops:
  0.7 32.2 %shard_map.55 = f32[64,128]{1,0:T(8,128)} custom-call(f32[64,128]{1,0:T(8,128)} %x_ref.1, s32[1,1,152]{2,1,0:T(1,128)} %rows_ref.1, s32[1,1,152]{2,1,0:T(1,128)} %cols_ref.1, s32[1,1]{1,0:T(1,128)S(6)} %copy.7.count_ref, bf16[1,1,152,128,128]{4,3,2,1,0:T(8,128)(2,1)} %blocks_ref.1), custom_call_target="tpu_custom_call" | custom-call | tf_op jit(solution)/shard_map/pallas_call | solution.py:362
  32.9 1.4 %copy.8 = f32[64,128]{1,0:T(8,128)} copy(f32[64,128]{1,0:T(8,128)} %shard_map.55) | data formatting | bytes 65536

commit v5 on v4

--- a/solution.py
+++ b/solution.py
@@ -89,86 +89,7 @@
             pltpu.make_async_copy(last_v, last_ref, chain_s.at[1]),
         )
 
-    barrier = pltpu.get_barrier_semaphore()
-
-    def greet(row, col):
-        pl.semaphore_signal(barrier, inc=1, device_id=(row, col), device_id_type=MESH)
-
-    for j in range(C):
-        @pl.when(j != b)
-        def _():
-            greet(a, j)
-    for i in range(R - 1):
-        @pl.when(i < a)
-        def _():
-            greet(i, my_col)
-    greeted = C - 1 + a
-    for h in range(G):
-        @pl.when(above(h))
-        def _():
-            for j in range(C):
-                greet(b + C * h, j)
-        greeted = greeted + jnp.where(above(h), C, 0)
-
-    @pl.when(live)
-    def _():
-        for copy in slot_copies():
-            copy.wait()
-        link_slots()
-        for copy in chain_copies():
-            copy.start()
-
-    pl.semaphore_wait(barrier, greeted)
-
-    def remote(src, dst, send, recv, row, col):
-        return pltpu.make_async_remote_copy(
-            src_ref=src, dst_ref=dst, send_sem=send, recv_sem=recv, device_id=(row, col), device_id_type=MESH
-        )
-
-    def send_x_col(t, v, i):
-        return remote(
-            wsend.at[t, v], xcol.at[t, v, my_group, b], xc_s.at[t, v, i], xc_r.at[t, v, my_group, b], i, my_col
-        )
-
-    def send_x_row(t, v, j):
-        return remote(wsend.at[t, v], xrow.at[t, v, b], xr_s.at[t, v, j], xr_r.at[t, v, b], a, j)
-
-    def send_col_term(t, v, h, j):
-        return remote(
-            csend.at[t, v, h, j], cterm.at[t, v, a], ct_s.at[t, v, h, j], ct_r.at[t, v, a], b + C * h, j
-        )
-
-    def send_row_term(t, v, j):
-        return remote(rsend.at[t, v, j], rterm.at[t, v, b], rt_s.at[t, v, j], rt_r.at[t, v, b], a, j)
-
-    def got_x_col(t, v, h, j):
-        remote(
-            wsend.at[t, v], xcol.at[t, v, h, j], xc_s.at[t, v, 0], xc_r.at[t, v, h, j], b + C * h, j
-        ).wait_recv()
-
-    def got_x_row(t, v, j):
-        remote(wsend.at[t, v], xrow.at[t, v, j], xr_s.at[t, v, j], xr_r.at[t, v, j], a, j).wait_recv()
-
-    def got_col_term(t, v, i):
-        remote(
-            csend.at[t, v, 0, 0], cterm.at[t, v, i], ct_s.at[t, v, 0, 0], ct_r.at[t, v, i], i, my_col
-        ).wait_recv()
-
-    def got_row_term(t, v, j):
-        remote(rsend.at[t, v, j], rterm.at[t, v, j], rt_s.at[t, v, j], rt_r.at[t, v, j], a, j).wait_recv()
-
-    def times(x, m):
-        return lax.dot_general(x, m, (((1,), (0,)), ((), ())), preferred_element_type=jnp.float32)
-
-    def times_t(x, m):
-        return lax.dot_general(x, m, (((1,), (1,)), ((), ())), preferred_element_type=jnp.float32)
-
-    def densify():
-        for copy in chain_copies():
-            copy.wait()
-        for part in sums:
-            part[0] = jnp.zeros(part.shape[1:], part.dtype)
-
+    def add_chunks(first, end):
         def chunk(k, carry):
             chunk_copy(k).wait()
             for n in range(per_chunk):
@@ -178,7 +99,22 @@
                     part[s + 1] = part[before] + buf[s, q * band : (q + 1) * band, :].astype(jnp.float32)
             return carry
 
-        lax.fori_loop(0, chunks, chunk, 0)
+        lax.fori_loop(first, end, chunk, 0)
+
+    def begin_dense():
+        for copy in slot_copies():
+            copy.wait()
+        link_slots()
+        for copy in chain_copies():
+            copy.start()
+        for part in sums:
+            part[0] = jnp.zeros(part.shape[1:], part.dtype)
+        for copy in chain_copies():
+            copy.wait()
+        add_chunks(0, chunks * 3 // 8)
+
+    def finish_dense():
+        add_chunks(chunks * 3 // 8, chunks)
 
         def store(n, carry):
             h, r = n // slab_blocks, n % slab_blocks
@@ -191,6 +127,76 @@
 
         lax.fori_loop(0, G * slab_blocks, store, 0)
 
+    barrier = pltpu.get_barrier_semaphore()
+
+    def greet(row, col):
+        pl.semaphore_signal(barrier, inc=1, device_id=(row, col), device_id_type=MESH)
+
+    for j in range(C):
+        @pl.when(j != b)
+        def _():
+            greet(a, j)
+    for i in range(R - 1):
+        @pl.when(i < a)
+        def _():
+            greet(i, my_col)
+    greeted = C - 1 + a
+    for h in range(G):
+        @pl.when(above(h))
+        def _():
+            for j in range(C):
+                greet(b + C * h, j)
+        greeted = greeted + jnp.where(above(h), C, 0)
+
+    @pl.when(live)
+    def _():
+        begin_dense()
+
+    pl.semaphore_wait(barrier, greeted)
+
+    def remote(src, dst, send, recv, row, col):
+        return pltpu.make_async_remote_copy(
+            src_ref=src, dst_ref=dst, send_sem=send, recv_sem=recv, device_id=(row, col), device_id_type=MESH
+        )
+
+    def send_x_col(t, v, i):
+        return remote(
+            wsend.at[t, v], xcol.at[t, v, my_group, b], xc_s.at[t, v, i], xc_r.at[t, v, my_group, b], i, my_col
+        )
+
+    def send_x_row(t, v, j):
+        return remote(wsend.at[t, v], xrow.at[t, v, b], xr_s.at[t, v, j], xr_r.at[t, v, b], a, j)
+
+    def send_col_term(t, v, h, j):
+        return remote(
+            csend.at[t, v, h, j], cterm.at[t, v, a], ct_s.at[t, v, h, j], ct_r.at[t, v, a], b + C * h, j
+        )
+
+    def send_row_term(t, v, j):
+        return remote(rsend.at[t, v, j], rterm.at[t, v, b], rt_s.at[t, v, j], rt_r.at[t, v, b], a, j)
+
+    def got_x_col(t, v, h, j):
+        remote(
+            wsend.at[t, v], xcol.at[t, v, h, j], xc_s.at[t, v, 0], xc_r.at[t, v, h, j], b + C * h, j
+        ).wait_recv()
+
+    def got_x_row(t, v, j):
+        remote(wsend.at[t, v], xrow.at[t, v, j], xr_s.at[t, v, j], xr_r.at[t, v, j], a, j).wait_recv()
+
+    def got_col_term(t, v, i):
+        remote(
+            csend.at[t, v, 0, 0], cterm.at[t, v, i], ct_s.at[t, v, 0, 0], ct_r.at[t, v, i], i, my_col
+        ).wait_recv()
+
+    def got_row_term(t, v, j):
+        remote(rsend.at[t, v, j], rterm.at[t, v, j], rt_s.at[t, v, j], rt_r.at[t, v, j], a, j).wait_recv()
+
+    def times(x, m):
+        return lax.dot_general(x, m, (((1,), (0,)), ((), ())), preferred_element_type=jnp.float32)
+
+    def times_t(x, m):
+        return lax.dot_general(x, m, (((1,), (1,)), ((), ())), preferred_element_type=jnp.float32)
+
     def side_by_side(ref, *index):
         return jnp.concatenate([ref[index + (j,)] for j in range(C)], axis=1)
 
@@ -279,7 +285,7 @@
 
     @pl.when(live)
     def _():
-        densify()
+        finish_dense()
 
     def sent_early(t):
         for v in range(V):
@@ -316,11 +322,15 @@
                 diagonal_terms(t, v)
             for v in range(V):
                 row_terms(t, v)
-        sent_early(t)
 
         @pl.when(t > 0)
         def _():
+            sent_early(t - 1)
             sent_late(t - 1)
+
+        @pl.when(t == DEGREE - 1)
+        def _():
+            sent_early(t)
 
         for v in range(V):
             update(t, v)

time: 34.5 us -> 35.2 us (1.020)
  Pallas kernels: 32.2 us -> 32.9 us
    pallas_call x1, Pallas kernels: 32.2 us -> 32.9 us  [local(): pl.pallas_call(functools.partial(filter_kernel, R, C, chunks), out_shape=...]
where the time goes in v5:
time: 35.2 us; the launch traced here: 35 us
  Pallas kernels  32.9 us (93%)
  local copies, waits for them, and re-layouts  1.38 us (4%)
  between operations  0.66 us (2%)
    pallas_call x1, Pallas kernels, local(): pl.pallas_call(functools.partial(filter_kernel, R, C, chunks), out_shape=...  32.9 us
    unnamed x1, local copies, waits for them, and re-layouts  1.38 us

profile of v5, /device:TPU:0, one launch (start us, length us, event | category | flops | bytes accessed | tf_op | source)
XLA Modules:
  0.0 35.0 jit_solution(1280739993260153727)
XLA Ops:
  0.7 32.9 %shard_map.55 = f32[64,128]{1,0:T(8,128)} custom-call(f32[64,128]{1,0:T(8,128)} %x_ref.1, s32[1,1,152]{2,1,0:T(1,128)} %rows_ref.1, s32[1,1,152]{2,1,0:T(1,128)} %cols_ref.1, s32[1,1]{1,0:T(1,128)S(6)} %copy.7.count_ref, bf16[1,1,152,128,128]{4,3,2,1,0:T(8,128)(2,1)} %blocks_ref.1), custom_call_target="tpu_custom_call" | custom-call | tf_op jit(solution)/shard_map/pallas_call | solution.py:372
  33.6 1.4 %copy.8 = f32[64,128]{1,0:T(8,128)} copy(f32[64,128]{1,0:T(8,128)} %shard_map.55) | data formatting | bytes 65536

commit v6 on v4

--- a/solution.py
+++ b/solution.py
@@ -197,14 +197,14 @@
     def hand_out(t, v):
         w = cur[v].astype(jnp.bfloat16)
         wsend[t, v] = w
+        for i in range(R - 1):
+            @pl.when(i < a)
+            def _():
+                send_x_col(t, v, i).start()
         for j in range(C):
             @pl.when((j != b) & alive(j))
             def _():
                 send_x_row(t, v, j).start()
-        for i in range(R - 1):
-            @pl.when(i < a)
-            def _():
-                send_x_col(t, v, i).start()
 
         @pl.when(live)
         def _():
@@ -316,11 +316,15 @@
                 diagonal_terms(t, v)
             for v in range(V):
                 row_terms(t, v)
-        sent_early(t)
 
         @pl.when(t > 0)
         def _():
+            sent_early(t - 1)
             sent_late(t - 1)
+
+        @pl.when(t == DEGREE - 1)
+        def _():
+            sent_early(t)
 
         for v in range(V):
             update(t, v)

time: 34.5 us -> 34.5 us (level)
  no operation moved by 1% of the time
where the time goes in v6:
time: 34.5 us; the launch traced here: 34.3 us
  Pallas kernels  32.3 us (94%)
  local copies, waits for them, and re-layouts  1.38 us (4%)
  between operations  0.66 us (2%)
    pallas_call x1, Pallas kernels, local(): pl.pallas_call(functools.partial(filter_kernel, R, C, chunks), out_shape=...  32.3 us
    unnamed x1, local copies, waits for them, and re-layouts  1.38 us

profile of v6, /device:TPU:0, one launch (start us, length us, event | category | flops | bytes accessed | tf_op | source)
XLA Modules:
  0.0 34.3 jit_solution(9787185726089776223)
XLA Ops:
  0.7 32.3 %shard_map.55 = f32[64,128]{1,0:T(8,128)} custom-call(f32[64,128]{1,0:T(8,128)} %x_ref.1, s32[1,1,152]{2,1,0:T(1,128)} %rows_ref.1, s32[1,1,152]{2,1,0:T(1,128)} %cols_ref.1, s32[1,1]{1,0:T(1,128)S(6)} %copy.7.count_ref, bf16[1,1,152,128,128]{4,3,2,1,0:T(8,128)(2,1)} %blocks_ref.1), custom_call_target="tpu_custom_call" | custom-call | tf_op jit(solution)/shard_map/pallas_call | solution.py:366
  32.9 1.4 %copy.8 = f32[64,128]{1,0:T(8,128)} copy(f32[64,128]{1,0:T(8,128)} %shard_map.55) | data formatting | bytes 65536
